TPU v7x, 256 devices: a whole 4x4x8 slice. The times are simulated.
256 devices in a mesh: cells: 256 (over y, x, z, core).
Axes of the slice: x: 4, y: 4, z: 8, core: 2. Of those that a mesh axis runs over, the one named last changes fastest.
Arguments:
- probes: bfloat16 [16, 64, 262144], P(None, None, 'cells'), may hold values from -6 to 6
- area: float32 [262144], P('cells'), may hold values from 1 to 30, as said below
- settle: float32 [16, 262144], P(None, 'cells'), may hold values from 0.05 to 0.5
- courant: float32 [3, 16, 262144], P(None, None, 'cells'), may hold values from 0.02 to 0.3
- orient: int32 [3, 16, 262144], P(None, None, 'cells'), may hold values from 0 to 1
- local_slot: int32 [3, 262144], P(None, 'cells'), may hold values from 0 to 1535, as said below
- send_rows: int32 [131072], P('cells'), may hold values from 0 to 1023, as said below
Outputs:
- basis: float32 [16, 64, 262144], P(None, None, 'cells')
- factor: float32 [64, 64], replicated
Inputs may be any that keep to these rules, and one draw needn't show every extreme that they name: `local_slot`: slot of the neighbour across face j of cell c in its device's table; a face whose slot is the cell itself is a closed boundary. The first device references no slot of the previous side and the last none of the next side. `send_rows`: entries 2 * 256 * d to 2 * 256 * (d + 1) - 1 are own-cell indices of device d: first the rows for device d - 1, then the rows for device d + 1; entries that no receiver's slot refers to are 0. `area`: areas are positive.
All inputs are finite; a program needn't handle non-finite values.
Results may differ from a plain program's by a relative error of at most 0.0014.
The roundings to bfloat16 on the way count: a program that leaves them out, or rounds other values in their place, can miss the bound.
Values may be sent and summed in bfloat16 or wider, within the bound.
A program may use at most 128 MiB of HBM per device.

v0:
```python
import jax
import jax.numpy as jnp
from jax import lax
from jax.sharding import PartitionSpec as P


def with_halo(array, sides, width):
    for axis, dim in sides:
        devices, length = (lax.axis_size(axis), array.shape[dim])
        up = [(i, (i + 1) % devices) for i in range(devices - 1)]
        down = [(j, i) for i, j in up]
        last = lax.slice_in_dim(array, length - width, length, axis=dim)
        initial = lax.slice_in_dim(array, 0, width, axis=dim)
        before = lax.ppermute(last, axis, up)
        after = lax.ppermute(initial, axis, down)
        array = jnp.concatenate([before, array, after], axis=dim)
    return array


def upper_factor(gram):
    width = gram.shape[0]
    index = jnp.arange(width, dtype=jnp.int32)

    def column(step, carry):
        rest, upper = carry
        pivot = jnp.sqrt(
            lax.dynamic_index_in_dim(
                lax.dynamic_index_in_dim(rest, step, 0, keepdims=False), step, 0, keepdims=False
            )
        )
        row_now = lax.dynamic_index_in_dim(rest, step, 0, keepdims=False) / pivot
        row_now = jnp.where(index >= step, row_now, jnp.zeros_like(row_now))
        rest = rest - row_now[:, None] * row_now[None, :]
        upper = lax.dynamic_update_index_in_dim(upper, row_now, step, 0)
        return (rest, upper)

    _, upper = lax.fori_loop(0, width, column, (gram, jnp.zeros_like(gram)))
    return upper


def upper_inverse(upper):
    width = upper.shape[0]
    identity = jnp.eye(width, dtype=upper.dtype)

    def row_step(turn, inverse):
        step = width - 1 - turn
        urow = lax.dynamic_index_in_dim(upper, step, 0, keepdims=False)
        pivot = lax.dynamic_index_in_dim(urow, step, 0, keepdims=False)
        known = jnp.dot(urow, inverse, precision=lax.Precision.HIGHEST)
        erow = lax.dynamic_index_in_dim(identity, step, 0, keepdims=False)
        return lax.dynamic_update_index_in_dim(inverse, (erow - known) / pivot, step, 0)

    return lax.fori_loop(0, width, row_step, jnp.zeros_like(upper))


def body(probes, area, settle, courant, orient, local_slot, send_rows):
    halo_rows = send_rows.shape[0] // 2
    lam = probes.astype(jnp.float32)
    scaled = (lam / area[None, None, :]).astype(jnp.bfloat16)
    outgoing = jnp.take(scaled, send_rows, axis=2)
    extended = with_halo(outgoing, (("cells", 2),), halo_rows)
    from_left = extended[:, :, :halo_rows]
    from_right = extended[:, :, 3 * halo_rows :]
    table = jnp.concatenate([scaled, from_left, from_right], axis=2)
    table = lax.optimization_barrier(table)
    below = jnp.concatenate([lam[1:], jnp.zeros_like(lam[:1])], axis=0)
    mu = lam + settle[:, None, :] * (below - lam)
    for face in range(3):
        other = jnp.take(table, local_slot[face], axis=2).astype(jnp.float32)
        weight = courant[face] * orient[face].astype(jnp.float32)
        mu = mu + weight[:, None, :] * (area[None, None, :] * other - lam)
    rows = jnp.sqrt(area)[None, None, :] * mu
    gram_local = jnp.einsum("lpc,lqc->pq", rows, rows, precision=lax.Precision.HIGHEST)
    upper_local = upper_factor(gram_local)
    stacked = lax.all_gather(upper_local[None], "cells", axis=0, tiled=True)
    gram = jnp.einsum("npq,npr->qr", stacked, stacked, precision=lax.Precision.HIGHEST)
    upper = upper_factor(gram)
    inverse = upper_inverse(upper)
    total_rows = rows.shape[0] * rows.shape[2] * lax.axis_size("cells")
    scale = jnp.sqrt(jnp.float32(total_rows))
    basis = jnp.einsum("qp,lqc->lpc", inverse, rows, precision=lax.Precision.HIGHEST) * scale
    return (basis, upper / scale)


def solution(mesh):
    in_specs = (
        P(None, None, "cells"),
        P("cells"),
        P(None, "cells"),
        P(None, None, "cells"),
        P(None, None, "cells"),
        P(None, "cells"),
        P("cells"),
    )
    out_specs = (P(None, None, "cells"), P())
    return jax.shard_map(body, mesh=mesh, in_specs=in_specs, out_specs=out_specs, check_vma=False)
```

profile of v0, /device:TPU:1, one launch (start us, length us, event | category | flops | bytes accessed | tf_op | source)
XLA Modules:
  0.0 561.7 jit_solution(15637968403709190937)
XLA Ops:
  8.6 2.3 fusion.17
  10.9 4.8 copy.38
  15.7 4.5 gather_fusion
  20.2 2.9 select_bitcast_fusion
  23.1 1.3 fusion.29
  24.5 2.8 copy.39
  27.2 4.9 collective-permute-start
  32.2 1.6 copy.40
  33.8 2.6 collective-permute-start.1
  36.5 2.4 slice.56
  39.0 5.7 %collective-permute-done.1 = bf16[16,64,256]{2,1,0:T(8,128)(2,1)S(1)} collective-permute-done((bf16[16,64,256]{2,1,0:T(8,128)(2,1)}, bf16[16,64,256]{2,1,0:T(8,128)(2,1)S(1)}, u32[]{:S(2)}, u32[]{:S(2)}) %collective-permute-start.1) | collective-permute-done | bytes 524320 | tf_op jit(solution)/shard_map/ppermute | solution.py:15
  44.7 3.1 pad_maximum_fusion
  47.8 8.6 %copy.41 = bf16[16,64,1536]{1,0,2:T(8,128)(2,1)} copy(bf16[16,64,1536]{2,1,0:T(8,128)(2,1)} %pad_maximum_fusion) | data formatting | bytes 6291456 | tf_op jit(solution)/shard_map/optimization_barrier | solution.py:65
  56.3 11.1 %gather_fusion.1 = bf16[1024,16,64]{2,1,0:T(8,128)(2,1)} fusion(bf16[16,64,1536]{1,0,2:T(8,128)(2,1)} %copy.41, s32[1024]{0:T(1024)S(1)} %fusion.26), kind=kCustom, calls=%fused_computation.clone | custom fusion | bytes 4198400 | tf_op jit(solution)/shard_map/jit(_take)/gather | solution.py:69
  67.4 5.5 copy.42
  72.8 11.1 %gather_fusion.2 = bf16[1024,16,64]{2,1,0:T(8,128)(2,1)} fusion(bf16[16,64,1536]{1,0,2:T(8,128)(2,1)} %copy.41, s32[1024]{0:T(1024)S(1)} %fusion.27), kind=kCustom, calls=%fused_computation.1.clone | custom fusion | bytes 4198400 | tf_op jit(solution)/shard_map/jit(_take)/gather | solution.py:69
  83.9 5.5 copy.44
  89.3 11.1 %gather_fusion.3 = bf16[1024,16,64]{2,1,0:T(8,128)(2,1)} fusion(bf16[16,64,1536]{1,0,2:T(8,128)(2,1)} %copy.41, s32[1024]{0:T(1024)S(1)} %fusion.28), kind=kCustom, calls=%fused_computation.2.clone | custom fusion | bytes 4198400 | tf_op jit(solution)/shard_map/jit(_take)/gather | solution.py:69
  100.4 5.5 copy.46
  106.0 5.7 %fusion.16 = f32[16,64,1024]{2,1,0:T(8,128)S(1)} fusion(bf16[16,64,1024]{2,1,0:T(8,128)(2,1)S(1)} %copy-done.1, f32[15,64,1024]{2,1,0:T(8,128)} %slice.56, bf16[1024,16,64]{0,2,1:T(8,128)(2,1)} %copy.46, bf16[1024,16,64]{0,2,1:T(8,128)(2,1)} %copy.44, bf16[1024,16,64]{0,2,1:T(8,128)(2,1)} %copy.42, f32[16,1024]{1,0:T(8,128)S(1)} %get-tuple-element.424, ...), kind=kLoop, calls=%fused_computation.33 | loop fusion | flops 24117248 | bytes 16788480 | tf_op jit(solution)/shard_map/mul | solution.py:72
  111.7 3.4 convolution_bitcast_fusion.1
  115.1 92.1 %while.55 = (s32[]{:T(128)}, f32[64,64]{1,0:T(8,128)S(1)}, f32[64,64]{1,0:T(8,128)S(1)}, s32[]{:T(128)}, s32[]{:T(128)}, /*index=5*/s32[]{:T(128)}) while((s32[]{:T(128)}, f32[64,64]{1,0:T(8,128)S(1)}, f32[64,64]{1,0:T(8,128)S(1)}, s32[]{:T(128)}, s32[]{:T(128)}, /*index=5*/s32[]{:T(128)}) %tuple.130), condition=%wide.region_1.3_spmd.clone, body=%wide.region_0.0_spmd.clone.sunk | while | flops 8643 | bytes 37237 | solution.py:37
  207.8 121.7 %all-gather.3.cloned.1.call-done = f32[16384,64]{1,0:T(8,128)} async-done(((f32[64,64]{1,0:T(8,128)}), f32[16384,64]{1,0:T(8,128)}) %all-gather.3.cloned.1.call-update) | async-done | bytes 4194320 | tf_op jit(solution)/shard_map/all_gather | solution.py:75
  329.6 30.7 %fusion.21 = f32[64,64]{1,0:T(8,128)S(1)} fusion(f32[256,64,64]{2,1,0:T(8,128)} %bitcast.98), kind=kOutput, calls=%fused_computation.41 | convolution fusion | flops 805306368 | bytes 4210688 | tf_op jit(solution)/shard_map/npq,npr->qr/dot_general | solution.py:76
  360.3 92.1 %while.56 = (s32[]{:T(128)}, f32[64,64]{1,0:T(8,128)S(1)}, f32[64,64]{1,0:T(8,128)S(1)}, s32[]{:T(128)}, s32[]{:T(128)}, /*index=5*/s32[]{:T(128)}) while((s32[]{:T(128)}, f32[64,64]{1,0:T(8,128)S(1)}, f32[64,64]{1,0:T(8,128)S(1)}, s32[]{:T(128)}, s32[]{:T(128)}, /*index=5*/s32[]{:T(128)}) %tuple.133), condition=%wide.region_3.5_spmd.clone, body=%wide.region_2.4_spmd.clone.sunk | while | flops 8643 | bytes 37237 | solution.py:37
  453.0 92.0 %while.54 = (s32[]{:T(128)}, f32[64,64]{1,0:T(8,128)S(1)}, f32[64,64]{1,0:T(8,128)S(1)}, f32[64,64]{1,0:T(8,128)S(1)}, s32[]{:T(128)}, /*index=5*/s32[]{:T(128)}, s32[]{:T(128)}, s32[]{:T(128)}) while((s32[]{:T(128)}, f32[64,64]{1,0:T(8,128)S(1)}, f32[64,64]{1,0:T(8,128)S(1)}, f32[64,64]{1,0:T(8,128)S(1)}, s32[]{:T(128)}, ...), condition=%wide.region_5.7_spmd, body=%wide.region_4.6_spmd.sunk | while | flops 49287 | bytes 35751 | solution.py:53
  453.6 0.8 fusion.44
  455.0 0.8 fusion.44
  456.5 0.8 fusion.44
  457.9 0.8 fusion.44
  459.3 0.8 fusion.44
  460.8 0.8 fusion.44
  462.2 0.8 fusion.44
  463.7 0.8 fusion.44
  465.1 0.8 fusion.44
  466.5 0.8 fusion.44
  468.0 0.8 fusion.44
  469.4 0.8 fusion.44
  470.9 0.8 fusion.44
  472.3 0.8 fusion.44
  473.7 0.8 fusion.44
  475.2 0.8 fusion.44
  476.6 0.8 fusion.44
  478.0 0.8 fusion.44
  479.5 0.8 fusion.44
  480.9 0.8 fusion.44
  482.4 0.8 fusion.44
  483.8 0.8 fusion.44
  485.2 0.8 fusion.44
  486.7 0.8 fusion.44
  488.1 0.8 fusion.44
  489.6 0.8 fusion.44
  491.0 0.8 fusion.44
  492.4 0.8 fusion.44
  493.9 0.8 fusion.44
  502.5 0.8 fusion.44
  503.9 0.8 fusion.44
  505.4 0.8 fusion.44
  506.8 0.8 fusion.44
  529.8 0.8 fusion.44
  531.3 0.8 fusion.44
  532.7 0.8 fusion.44
  534.1 0.8 fusion.44
  545.0 9.8 %multiply_bitcast_fusion = f32[16,64,1024]{2,1,0:T(8,128)} fusion(f32[16,64,1024]{2,1,0:T(8,128)} %copy-done, f32[64,64]{1,0:T(8,128)S(1)} %get-tuple-element.380), kind=kOutput, calls=%fused_computation.38 | convolution fusion | flops 806354944 | bytes 8404992 | tf_op jit(solution)/shard_map/qp,lqc->lpc/dot_general | solution.py:81
  (960 shorter events, 157.3 us)
Async XLA Ops:
  7.2 322.4 %all-gather.3.cloned.1.call-start = ((), (), s32[]{:S(2)}) async-start(), calls=%async_computation | async-start | bytes 8421376 | tf_op jit(solution)/shard_map/all_gather | solution.py:75
  10.8 9.4 %copy-start.2 = (bf16[16,64,1024]{2,1,0:T(8,128)(2,1)}, bf16[16,64,1024]{2,1,0:T(8,128)(2,1)S(1)}, u32[]{:S(2)}) copy-start(bf16[16,64,1024]{2,1,0:T(8,128)(2,1)S(1)} %fusion.17) | copy-start | bytes 6291460
  23.1 13.3 %copy-start.8 = (s32[3,1024]{1,0:T(4,128)S(1)}, s32[3,1024]{1,0:T(4,128)}, u32[]{:S(2)}) copy-start(s32[3,1024]{1,0:T(4,128)} %param.20) | copy-start | bytes 36868
  23.1 13.4 %copy-start.1 = (bf16[16,64,1024]{2,1,0:T(8,128)(2,1)S(1)}, bf16[16,64,1024]{2,1,0:T(8,128)(2,1)}, u32[]{:S(2)}) copy-start(bf16[16,64,1024]{2,1,0:T(8,128)(2,1)} %param.15) | copy-start | bytes 6291460
  27.2 11.7 %collective-permute-start = (bf16[16,64,256]{2,1,0:T(8,128)(2,1)}, bf16[16,64,256]{2,1,0:T(8,128)(2,1)}, u32[]{:S(2)}, u32[]{:S(2)}) collective-permute-start(bf16[16,64,256]{2,1,0:T(8,128)(2,1)} %copy.39), channel_id=1, source_target_pairs={{0,1},{1,2},{2,3},{3,4},{4,5},{5,6},{6,7},{7,8},{8,9},{9,10},{10,1... | collective-permute-start | bytes 1572872 | tf_op jit(solution)/shard_map/ppermute | solution.py:14
  33.8 5.1 copy-start.7
  33.8 5.1 copy-start.3
  33.8 5.1 copy-start.4
  33.8 10.8 %collective-permute-start.1 = (bf16[16,64,256]{2,1,0:T(8,128)(2,1)}, bf16[16,64,256]{2,1,0:T(8,128)(2,1)S(1)}, u32[]{:S(2)}, u32[]{:S(2)}) collective-permute-start(bf16[16,64,256]{2,1,0:T(8,128)(2,1)} %copy.40), channel_id=1, source_target_pairs={{1,0},{2,1},{3,2},{4,3},{5,4},{6,5},{7,6},{8,7},{9,8},{10,9},{11,1... | collective-permute-start | bytes 1572872 | tf_op jit(solution)/shard_map/ppermute | solution.py:15
  100.4 5.5 copy-start.6
  111.7 3.4 copy-start
  207.2 0.6 copy-start.5
Sparse Core Ops, SparseCore 0:
  207.9 121.5 all-gather.2
where the time goes:
time: 566 us; the launch traced here: 562 us
  local copies, waits for them, and re-layouts  198 us (35%)
  waiting for transfers between devices  127 us (22%)
  loops' own time  93.5 us (17%)
  matrix products  92.7 us (16%)
  other arithmetic  28.4 us (5%)
  between operations  14.3 us (3%)
  starting transfers between devices  7.56 us (1%)
    all_gather x1, waiting for transfers between devices, body(): stacked = lax.all_gather(upper_local[None], 'cells', axis=0, tiled=True)  122 us
    another operation x2, loops' own time, upper_factor(): _, upper = lax.fori_loop(0, width, column, (gram, jnp.zeros_like(gram)))  91.8 us
    dynamic_slice x128, local copies, waits for them, and re-layouts, column(): lax.dynamic_index_in_dim(lax.dynamic_index_in_dim(rest, step, 0, keepdims...  75.2 us
    gather x6, local copies, waits for them, and re-layouts, body(): other = jnp.take(table, local_slot[face], axis=2).astype(jnp.float32)  49.6 us
    dot_general x64, matrix products, row_step(): known = jnp.dot(urow, inverse, precision=lax.Precision.HIGHEST)  48.9 us
    dynamic_slice x64, local copies, waits for them, and re-layouts, row_step(): pivot = lax.dynamic_index_in_dim(urow, step, 0, keepdims=False)  39.8 us
    dot_general x1, matrix products, body(): jnp.einsum('npq,npr->qr', stacked, stacked, precision=lax.Precision.HIGHEST)  30.7 us
  transfers between devices with their start and end apart: 3, of which 2 were waited for; matrix products, arithmetic and copies ran while one was open for 1% of the time, Pallas kernels for 0%

commit v1 on v0

v1 whole, which is shorter than its diff:
```python
import functools
import math

import jax
import jax.numpy as jnp
from jax import lax
from jax.experimental import pallas as pl
from jax.experimental.pallas import tpu as pltpu
from jax.sharding import PartitionSpec as P

MESH = pl.DeviceIdType.MESH
GROUP = 16
TILE = 256
NT = (((1,), (1,)), ((), ()))


def advect_kernel(
    devices, probes, area, settle, courant, orient, slots, sends, pairs_out, gram_out,
    v, outgoing, ghosts, total, pairs, parts, recv_a, recv_b, recv_c,
    halo_send, halo_recv, send_sem, recv_sem, store_sem,
):
    layers, cells = settle.shape
    width = probes.shape[0] // layers
    halo = ghosts.shape[2]
    chunks = probes.shape[0] // TILE
    others = devices // GROUP
    me = lax.axis_index("cells")
    left, right = lax.rem(me + devices - 1, devices), lax.rem(me + 1, devices)
    place = lax.rem(me, GROUP)
    base = me - place
    block = me // GROUP

    barrier = pltpu.get_barrier_semaphore()
    for side in (left, right):
        pl.semaphore_signal(barrier, inc=1, device_id=(side,), device_id_type=MESH)

    def greet(step, _):
        near = base + lax.rem(place + step, GROUP)
        far = lax.rem(block + step, others) * GROUP + place
        pl.semaphore_signal(barrier, inc=1, device_id=(near,), device_id_type=MESH)
        pl.semaphore_signal(barrier, inc=1, device_id=(far,), device_id_type=MESH)
        return 0

    lax.fori_loop(1, GROUP, greet, 0)

    one, zero = jnp.bfloat16(1), jnp.bfloat16(0)
    cell_area = area[...]
    inverse_area = 1.0 / cell_area
    pick = jnp.where(
        lax.broadcasted_iota(jnp.int32, (cells, 2 * halo), 0) == sends[...], one, zero
    )
    copies = []
    for chunk in range(chunks):
        rows = pl.ds(chunk * TILE, TILE)
        part = (probes[rows, :].astype(jnp.float32) * inverse_area).astype(jnp.bfloat16)
        v[rows, :] = part
        picked = jnp.dot(part, pick, preferred_element_type=jnp.float32).astype(jnp.bfloat16)
        outgoing[0, rows, :] = picked[:, :halo]
        outgoing[1, rows, :] = picked[:, halo:]
        if chunk == 0:
            pl.semaphore_wait(barrier, 2 * GROUP)
        for side, target in ((0, left), (1, right)):
            copy = pltpu.make_async_remote_copy(
                src_ref=outgoing.at[side, rows, :],
                dst_ref=ghosts.at[1 - side, rows, :],
                send_sem=halo_send.at[side, chunk],
                recv_sem=halo_recv.at[1 - side, chunk],
                device_id=(target,),
                device_id_type=MESH,
            )
            copy.start()
            copies.append(copy)

    root = jnp.sqrt(cell_area)
    settled = settle[...]
    weights = [courant[face] * orient[face].astype(jnp.float32) for face in range(3)]
    keep = root * (1.0 - settled - weights[0] - weights[1] - weights[2])
    fall = root * settled
    grown = root * cell_area
    fluxes = [grown * weight for weight in weights]

    for tile in range(cells // TILE):
        columns = pl.ds(tile * TILE, TILE)
        here = slice(tile * TILE, (tile + 1) * TILE)
        for face in range(3):
            hot = jnp.where(
                lax.broadcasted_iota(jnp.int32, (cells, TILE), 0) == slots[pl.ds(face, 1), columns],
                one, zero,
            )
            other = jnp.dot(v[...], hot, preferred_element_type=jnp.float32)
            for layer in range(layers):
                rows = pl.ds(layer * width, width)
                term = fluxes[face][layer : layer + 1, here] * other[layer * width : (layer + 1) * width]
                if face == 0:
                    lam = probes[rows, columns].astype(jnp.float32)
                    term = term + keep[layer : layer + 1, here] * lam
                    if layer < layers - 1:
                        lower = probes[pl.ds((layer + 1) * width, width), columns]
                        term = term + fall[layer : layer + 1, here] * lower.astype(jnp.float32)
                    total[rows, columns] = term
                else:
                    total[rows, columns] += term

    for chunk in range(chunks):
        for side in range(2):
            rows = pl.ds(chunk * TILE, TILE)
            pltpu.make_async_remote_copy(
                src_ref=outgoing.at[side, rows, :],
                dst_ref=ghosts.at[side, rows, :],
                send_sem=halo_send.at[side, chunk],
                recv_sem=halo_recv.at[side, chunk],
                device_id=(right,),
                device_id_type=MESH,
            ).wait_recv()

    for tile in range(cells // TILE):
        columns = pl.ds(tile * TILE, TILE)
        here = slice(tile * TILE, (tile + 1) * TILE)
        for face in range(3):
            place_of = slots[pl.ds(face, 1), columns] - cells
            other = None
            for side in range(2):
                hot = jnp.where(
                    lax.broadcasted_iota(jnp.int32, (halo, TILE), 0) + side * halo == place_of, one, zero
                )
                product = jnp.dot(ghosts[side], hot, preferred_element_type=jnp.float32)
                other = product if other is None else other + product
            for layer in range(layers):
                rows = pl.ds(layer * width, width)
                term = fluxes[face][layer : layer + 1, here] * other[layer * width : (layer + 1) * width]
                term = total[rows, columns] + term
                if face < 2:
                    total[rows, columns] = term
                else:
                    high = term.astype(jnp.bfloat16)
                    low = (term - high.astype(jnp.float32)).astype(jnp.bfloat16)
                    pairs[layer // 2, pl.ds((layer % 2) * 2 * width, width), columns] = high
                    pairs[layer // 2, pl.ds((layer % 2) * 2 * width + width, width), columns] = low

    stores = []
    for pair in range(layers // 2):
        copy = pltpu.make_async_copy(pairs.at[pair], pairs_out.at[pair], store_sem.at[pair])
        copy.start()
        stores.append(copy)

    square = None
    for pair in range(layers // 2):
        rows = pairs[pair]
        product = lax.dot_general(rows, rows, NT, preferred_element_type=jnp.float32)
        square = product if square is None else square + product
    w = width
    gram = None
    for layer in range(2):
        for a in range(2):
            for b in range(2):
                r, c = (2 * layer + a) * w, (2 * layer + b) * w
                piece = square[r : r + w, c : c + w]
                gram = piece if gram is None else gram + piece
    folded = jnp.concatenate([gram[: w // 2], gram[w // 2 :]], axis=1)
    lines = parts.shape[1]
    for index in range(GROUP):
        parts[index] = folded[index * lines : (index + 1) * lines]

    def exchange(phase, source, target_of, receive, slot):
        def begin(step, _):
            pltpu.make_async_remote_copy(
                src_ref=source(step),
                dst_ref=receive.at[slot],
                send_sem=send_sem.at[phase],
                recv_sem=recv_sem.at[phase],
                device_id=(target_of(step),),
                device_id_type=MESH,
            ).start()
            return 0

        lax.fori_loop(1, GROUP, begin, 0)
        everything = receive.at[pl.ds(0, GROUP - 1)]
        pltpu.make_async_copy(everything, everything, recv_sem.at[phase]).wait()

    def near(step):
        return base + lax.rem(place + step, GROUP)

    def far(step):
        return lax.rem(block + step, others) * GROUP + place

    def add_up(receive):
        terms = [receive[index] for index in range(GROUP)]
        while len(terms) > 1:
            terms = [a + b for a, b in zip(terms[::2], terms[1::2])]
        return terms[0]

    exchange(0, lambda step: parts.at[lax.rem(place + step, GROUP)], near, recv_a, place)
    recv_a[place] = parts[place]
    recv_b[block] = add_up(recv_a)
    exchange(1, lambda step: recv_b.at[block], far, recv_b, block)
    recv_c[place] = add_up(recv_b)
    exchange(2, lambda step: recv_c.at[place], near, recv_c, place)
    gram_out[...] = recv_c[...]

    for phase, buffer in ((0, recv_a), (1, recv_b), (2, recv_c)):
        everything = buffer.at[pl.ds(0, GROUP - 1)]
        pltpu.make_async_copy(everything, everything, send_sem.at[phase]).wait()
    for copy in copies:
        copy.wait_send()
    for copy in stores:
        copy.wait()


def basis_kernel(scale, pairs, gram, basis, factor, loaded, finished, load_sem, store_sem):
    groups = pairs.shape[0]
    width = factor.shape[0]
    loads = []
    for group in range(groups):
        copy = pltpu.make_async_copy(pairs.at[group], loaded.at[group], load_sem.at[group])
        copy.start()
        loads.append(copy)

    folded = jnp.concatenate([gram[index] for index in range(gram.shape[0])], axis=0)
    whole = jnp.concatenate([folded[:, :width], folded[:, width:]], axis=0)
    row = lax.broadcasted_iota(jnp.int32, (width, 2 * width), 0)
    lane = lax.broadcasted_iota(jnp.int32, (width, 2 * width), 1)
    unit = (lax.broadcasted_iota(jnp.int32, (width, width), 0)
            == lax.broadcasted_iota(jnp.int32, (width, width), 1)).astype(jnp.float32)
    work = jnp.concatenate([whole, unit], axis=1)
    strips = [work[8 * i : 8 * i + 8] for i in range(width // 8)]
    low_row = lax.broadcasted_iota(jnp.int32, (8, 1), 0)
    for step in range(width):
        home, inner = step // 8, step % 8
        line = strips[home][inner : inner + 1]
        line = line * (1.0 / line[:, step : step + 1])
        for strip in range(home, width // 8):
            column = strips[strip][:, step : step + 1]
            if strip == home:
                column = jnp.where(low_row > inner, column, 0.0)
            strips[strip] = strips[strip] - column * line
    work = jnp.concatenate(strips, axis=0)
    pivots = jnp.sum(jnp.where(lane == row, work, 0.0), axis=1, keepdims=True)
    work = work / jnp.sqrt(pivots)
    factor[...] = jnp.where(lane >= row, work, 0.0)[:, :width] / scale
    inverse = jnp.where(lane - width <= row, work, 0.0)[:, width:] * scale
    high = inverse.astype(jnp.bfloat16)
    low = (inverse - high.astype(jnp.float32)).astype(jnp.bfloat16)
    none = jnp.zeros_like(high)

    def spread(block):
        return jnp.concatenate([
            jnp.concatenate([block, block, none, none], axis=1),
            jnp.concatenate([none, none, block, block], axis=1),
        ], axis=0)

    lead, rest = spread(high), spread(low)
    stores = []
    for group in range(groups):
        loads[group].wait()
        rows = loaded[group]
        result = jnp.dot(lead, rows, preferred_element_type=jnp.float32)
        result += jnp.dot(rest, rows, preferred_element_type=jnp.float32)
        finished[group] = result
        copy = pltpu.make_async_copy(finished.at[group], basis.at[group], store_sem.at[group])
        copy.start()
        stores.append(copy)
    for copy in stores:
        copy.wait()


def body(probes, area, settle, courant, orient, local_slot, send_rows):
    layers, width, cells = probes.shape
    halo = send_rows.shape[0] // 2
    devices = lax.axis_size("cells")
    groups = layers // 2
    lines = width * width // (GROUP * 2 * width)
    vmem = pl.BlockSpec(memory_space=pltpu.VMEM)
    anywhere = pl.BlockSpec(memory_space=pl.ANY)
    chunks = layers * width // TILE
    flat = probes.reshape(layers * width, cells)
    pairs, gram = pl.pallas_call(
        functools.partial(advect_kernel, devices),
        out_shape=(
            jax.ShapeDtypeStruct((groups, 4 * width, cells), jnp.bfloat16),
            jax.ShapeDtypeStruct((GROUP, lines, 2 * width), jnp.float32),
        ),
        in_specs=[vmem] * 7,
        out_specs=(anywhere, vmem),
        scratch_shapes=[
            pltpu.VMEM((layers * width, cells), jnp.bfloat16),
            pltpu.VMEM((2, layers * width, halo), jnp.bfloat16),
            pltpu.VMEM((2, layers * width, halo), jnp.bfloat16),
            pltpu.VMEM((layers * width, cells), jnp.float32),
            pltpu.VMEM((groups, 4 * width, cells), jnp.bfloat16),
            pltpu.VMEM((GROUP, lines, 2 * width), jnp.float32),
            pltpu.VMEM((GROUP, lines, 2 * width), jnp.float32),
            pltpu.VMEM((GROUP, lines, 2 * width), jnp.float32),
            pltpu.VMEM((GROUP, lines, 2 * width), jnp.float32),
            pltpu.SemaphoreType.DMA((2, chunks)),
            pltpu.SemaphoreType.DMA((2, chunks)),
            pltpu.SemaphoreType.DMA((3,)),
            pltpu.SemaphoreType.DMA((3,)),
            pltpu.SemaphoreType.DMA((groups,)),
        ],
        compiler_params=pltpu.CompilerParams(
            collective_id=0, has_side_effects=True, vmem_limit_bytes=44 * 2**20
        ),
        name="advect",
    )(flat, area[None, :], settle, courant, orient, local_slot, send_rows[None, :])
    scale = math.sqrt(layers * cells * devices)
    basis, factor = pl.pallas_call(
        functools.partial(basis_kernel, scale),
        out_shape=(
            jax.ShapeDtypeStruct((groups, 2 * width, cells), jnp.float32),
            jax.ShapeDtypeStruct((width, width), jnp.float32),
        ),
        in_specs=[anywhere, vmem],
        out_specs=(anywhere, vmem),
        scratch_shapes=[
            pltpu.VMEM((groups, 4 * width, cells), jnp.bfloat16),
            pltpu.VMEM((groups, 2 * width, cells), jnp.float32),
            pltpu.SemaphoreType.DMA((groups,)),
            pltpu.SemaphoreType.DMA((groups,)),
        ],
        compiler_params=pltpu.CompilerParams(vmem_limit_bytes=24 * 2**20),
        name="basis",
    )(pairs, gram)
    return basis.reshape(layers, width, cells), factor


def solution(mesh):
    in_specs = (
        P(None, None, "cells"),
        P("cells"),
        P(None, "cells"),
        P(None, None, "cells"),
        P(None, None, "cells"),
        P(None, "cells"),
        P("cells"),
    )
    out_specs = (P(None, None, "cells"), P())
    return jax.shard_map(body, mesh=mesh, in_specs=in_specs, out_specs=out_specs, check_vma=False)
```

time: 566 us -> 58.1 us (0.10)
  local copies, waits for them, and re-layouts: 198 us -> 6.36 us
  waiting for transfers between devices: 127 us -> 0 us
  loops' own time: 93.5 us -> 0 us
  matrix products: 92.7 us -> 0 us
  Pallas kernels: 0 us -> 50.6 us
  other arithmetic: 28.4 us -> 0 us
  between operations: 14.3 us -> 0.82 us
  starting transfers between devices: 7.56 us -> 0 us
    all_gather x1 -> x0, waiting for transfers between devices: 122 us -> none  [body(): stacked = lax.all_gather(upper_local[None], 'cells', axis=0, tiled=True)]
    dynamic_slice x192 -> x0, local copies, waits for them, and re-layouts: 115 us -> none  [the longest x128 75.2 us: column(): lax.dynamic_index_in_dim(lax.dynamic_index_in_dim(rest, step, 0, keepdims...]
    another operation x3 -> x0, loops' own time: 93.5 us -> none  [the longest x2 91.8 us: upper_factor(): _, upper = lax.fori_loop(0, width, column, (gram, jnp.zeros_like(gram)))]
    dot_general x67 -> x0, matrix products: 92.7 us -> none  [the longest x64 48.9 us: row_step(): known = jnp.dot(urow, inverse, precision=lax.Precision.HIGHEST)]
    gather x7 -> x0, local copies, waits for them, and re-layouts: 54.2 us -> none  [the longest x6 49.6 us: body(): other = jnp.take(table, local_slot[face], axis=2).astype(jnp.float32)]
    pallas_call x0 -> x2, Pallas kernels: none -> 50.6 us  [the longest x1 40.6 us: body(): pl.pallas_call(functools.partial(advect_kernel, devices), out_shape=(jax....]
    sub x128 -> x0, other arithmetic: 9.7 us -> none  [column(): rest = rest - row_now[:, None] * row_now[None, :]]
    optimization_barrier x1 -> x0, local copies, waits for them, and re-layouts: 8.55 us -> none  [body(): table = lax.optimization_barrier(table)]
  transfers between devices with their start and end apart: 3 -> 0, of which waited for: 2 -> 0; matrix products, arithmetic and copies ran while one was open for 1% -> 0% of each run, Pallas kernels for 0% -> 0%
where the time goes in v1:
time: 58.1 us; the launch traced here: 57.8 us
  Pallas kernels  50.6 us (87%)
  local copies, waits for them, and re-layouts  6.36 us (11%)
  between operations  0.82 us (1%)
    pallas_call x1, Pallas kernels, body(): pl.pallas_call(functools.partial(advect_kernel, devices), out_shape=(jax....  40.6 us
    pallas_call x1, Pallas kernels, body(): pl.pallas_call(functools.partial(basis_kernel, scale), out_shape=(jax.Sha...  10.1 us
    unnamed x14, local copies, waits for them, and re-layouts  6.36 us

profile of v1, /device:TPU:1, one launch (start us, length us, event | category | flops | bytes accessed | tf_op | source)
XLA Modules:
  0.0 57.8 jit_solution(12766489214250762822)
XLA Ops:
  0.6 0.0 copy-start
  0.6 1.6 %copy-done = bf16[16,64,1024]{2,1,0:T(8,128)(2,1)S(1)} copy-done((bf16[16,64,1024]{2,1,0:T(8,128)(2,1)S(1)}, bf16[16,64,1024]{2,1,0:T(8,128)(2,1)}, u32[]{:S(2)}) %copy-start) | copy-done | bytes 2097176
  2.2 0.0 copy-start.1
  2.2 0.9 %copy-done.1 = f32[3,16,1024]{2,1,0:T(8,128)S(1)} copy-done((f32[3,16,1024]{2,1,0:T(8,128)S(1)}, f32[3,16,1024]{2,1,0:T(8,128)}, u32[]{:S(2)}) %copy-start.1) | copy-done | bytes 196632
  3.2 0.0 copy-start.2
  3.2 0.9 %copy-done.2 = s32[3,16,1024]{2,1,0:T(8,128)S(1)} copy-done((s32[3,16,1024]{2,1,0:T(8,128)S(1)}, s32[3,16,1024]{2,1,0:T(8,128)}, u32[]{:S(2)}) %copy-start.2) | copy-done | bytes 196632
  4.1 0.0 copy-start.3
  4.1 0.8 %copy-done.3 = f32[16,1024]{1,0:T(8,128)S(1)} copy-done((f32[16,1024]{1,0:T(8,128)S(1)}, f32[16,1024]{1,0:T(8,128)}, u32[]{:S(2)}) %copy-start.3) | copy-done | bytes 65560
  4.9 0.0 copy-start.4
  4.9 0.7 %copy-done.4 = s32[3,1024]{1,0:T(4,128)S(1)} copy-done((s32[3,1024]{1,0:T(4,128)S(1)}, s32[3,1024]{1,0:T(4,128)}, u32[]{:S(2)}) %copy-start.4) | copy-done | bytes 12312
  5.6 0.0 copy-start.5
  5.6 0.7 %copy-done.5 = f32[1024]{0:T(1024)S(1)} copy-done((f32[1024]{0:T(1024)S(1)}, f32[1024]{0:T(1024)}, u32[]{:S(2)}) %copy-start.5) | copy-done | bytes 4120
  6.3 0.0 copy-start.6
  6.3 0.7 %copy-done.6 = s32[512]{0:T(512)S(1)} copy-done((s32[512]{0:T(512)S(1)}, s32[512]{0:T(512)}, u32[]{:S(2)}) %copy-start.6) | copy-done | bytes 2072
  7.0 40.6 %advect.1 = (bf16[8,256,1024]{2,1,0:T(8,128)(2,1)S(1)}, f32[16,2,128]{2,1,0:T(2,128)S(1)}) custom-call(bf16[1024,1024]{1,0:T(8,128)(2,1)S(1)} %bitcast.4, f32[1,1024]{1,0:T(1,128)S(1)} %bitcast.5, f32[16,1024]{1,0:T(8,128)S(1)} %copy-done.3, f32[3,16,1024]{2,1,0:T(8,128)S(1)} %copy-done.1, s32[3,16,1024]{2,1,0:T(8,128)S(1)} %copy-done.2, ...), custom_call_target="tpu_custom_call" | custom-call | tf_op jit(solution)/shard_map/advect/pallas_call | solution.py:276
  47.6 10.1 %basis.1 = (f32[8,128,1024]{2,1,0:T(8,128)}, f32[64,64]{1,0:T(8,128)}) custom-call(bf16[8,256,1024]{2,1,0:T(8,128)(2,1)S(1)} %get-tuple-element.6.pairs, f32[16,2,128]{2,1,0:T(2,128)S(1)} %get-tuple-element.7.gram), custom_call_target="tpu_custom_call" | custom-call | tf_op jit(solution)/shard_map/basis/pallas_call | solution.py:306
Async XLA Ops:
  0.6 1.6 %copy-start = (bf16[16,64,1024]{2,1,0:T(8,128)(2,1)S(1)}, bf16[16,64,1024]{2,1,0:T(8,128)(2,1)}, u32[]{:S(2)}) copy-start(bf16[16,64,1024]{2,1,0:T(8,128)(2,1)} %param.7) | copy-start | bytes 6291460
  2.2 0.9 %copy-start.1 = (f32[3,16,1024]{2,1,0:T(8,128)S(1)}, f32[3,16,1024]{2,1,0:T(8,128)}, u32[]{:S(2)}) copy-start(f32[3,16,1024]{2,1,0:T(8,128)} %courant.1) | copy-start | bytes 589828
  3.2 0.9 %copy-start.2 = (s32[3,16,1024]{2,1,0:T(8,128)S(1)}, s32[3,16,1024]{2,1,0:T(8,128)}, u32[]{:S(2)}) copy-start(s32[3,16,1024]{2,1,0:T(8,128)} %orient.1) | copy-start | bytes 589828
  4.1 0.8 %copy-start.3 = (f32[16,1024]{1,0:T(8,128)S(1)}, f32[16,1024]{1,0:T(8,128)}, u32[]{:S(2)}) copy-start(f32[16,1024]{1,0:T(8,128)} %settle.1) | copy-start | bytes 196612
  4.9 0.7 %copy-start.4 = (s32[3,1024]{1,0:T(4,128)S(1)}, s32[3,1024]{1,0:T(4,128)}, u32[]{:S(2)}) copy-start(s32[3,1024]{1,0:T(4,128)} %slots.1) | copy-start | bytes 36868
  5.6 0.7 %copy-start.5 = (f32[1024]{0:T(1024)S(1)}, f32[1024]{0:T(1024)}, u32[]{:S(2)}) copy-start(f32[1024]{0:T(1024)} %param.8) | copy-start | bytes 12292
  6.3 0.7 %copy-start.6 = (s32[512]{0:T(512)S(1)}, s32[512]{0:T(512)}, u32[]{:S(2)}) copy-start(s32[512]{0:T(512)} %param.13) | copy-start | bytes 6148

commit v2 on v1

v2 whole, which is shorter than its diff:
```python
import functools
import itertools
import math

import jax
import jax.numpy as jnp
from jax import lax
from jax.experimental import pallas as pl
from jax.experimental.pallas import tpu as pltpu
from jax.sharding import PartitionSpec as P

MESH = pl.DeviceIdType.MESH
Y, X, Z = 4, 4, 8
CHUNK = 512
NT = (((1,), (1,)), ((), ()))


def far_first(*sizes):
    offsets = itertools.product(*(range(size) for size in sizes))
    away = lambda offset: sum(min(o, s - o) for o, s in zip(offset, sizes))
    ordered = sorted((o for o in offsets if any(o)), key=away, reverse=True)
    return ordered if len(sizes) > 1 else [o for o, in ordered]


def advect_kernel(
    devices, probes_in, area_in, settle_in, courant_in, orient_in, slots_in, sends_in,
    pairs, gram_out,
    probes, area, settle, courant, orient, slots, sends,
    v, outgoing, ghosts, total, halves, from_core, along_z, along_xy, final,
    load_sem, halo_send, halo_recv, send_sem, recv_sem,
):
    layers, cells = settle.shape
    width = probes.shape[0] // layers
    halo = sends.shape[1] // 2
    chunks = probes.shape[0] // CHUNK
    me = lax.axis_index("cells")
    left, right = lax.rem(me + devices - 1, devices), lax.rem(me + 1, devices)
    core, z, block = lax.rem(me, 2), lax.rem(me // 2, Z), me // (2 * Z)
    y, x = block // X, lax.rem(block, X)
    sibling = me + 1 - 2 * core
    z_peers = [me + 2 * (lax.rem(z + step, Z) - z) for step in far_first(Z)]
    xy_peers = [
        (lax.rem(y + dy, Y) * X + lax.rem(x + dx, X)) * 2 * Z + z * 2 + core
        for dy, dx in far_first(Y, X)
    ]

    loads = {}
    for index, (name, source, target) in enumerate((
        ("sends", sends_in, sends), ("area", area_in, area), ("probes", probes_in, probes),
        ("slots", slots_in, slots), ("courant", courant_in, courant),
        ("orient", orient_in, orient), ("settle", settle_in, settle),
    )):
        loads[name] = pltpu.make_async_copy(source, target, load_sem.at[index])
        loads[name].start()

    barrier = pltpu.get_barrier_semaphore()
    greeted = [left, right, sibling] + z_peers + xy_peers
    for peer in greeted:
        pl.semaphore_signal(barrier, inc=1, device_id=(peer,), device_id_type=MESH)

    one, zero = jnp.bfloat16(1), jnp.bfloat16(0)
    loads["sends"].wait()
    pick = jnp.where(
        lax.broadcasted_iota(jnp.int32, (cells, 2 * halo), 0) == sends[...], one, zero
    )
    loads["area"].wait()
    cell_area = area[...]
    inverse_area = 1.0 / cell_area
    loads["probes"].wait()
    copies, arrivals = [], []
    for chunk in range(chunks):
        rows = pl.ds(chunk * CHUNK, CHUNK)
        part = (probes[rows, :].astype(jnp.float32) * inverse_area).astype(jnp.bfloat16)
        v[rows, :] = part
        picked = jnp.dot(part, pick, preferred_element_type=jnp.float32).astype(jnp.bfloat16)
        outgoing[0, rows, :] = picked[:, :halo]
        outgoing[1, rows, :] = picked[:, halo:]
        if chunk == 0:
            pl.semaphore_wait(barrier, len(greeted))
        for side, target in ((0, left), (1, right)):
            copy = pltpu.make_async_remote_copy(
                src_ref=outgoing.at[side, rows, :],
                dst_ref=ghosts.at[rows, pl.ds((1 - side) * halo, halo)],
                send_sem=halo_send.at[side, chunk],
                recv_sem=halo_recv.at[1 - side, chunk],
                device_id=(target,),
                device_id_type=MESH,
            )
            copy.start()
            copies.append(copy)
            arrivals.append(pltpu.make_async_copy(
                outgoing.at[side, rows, :], ghosts.at[rows, pl.ds(side * halo, halo)], halo_recv.at[side, chunk]
            ))

    for name in ("slots", "courant", "orient", "settle"):
        loads[name].wait()
    root = jnp.sqrt(cell_area)
    settled = settle[...]
    weights = [courant[face] * orient[face].astype(jnp.float32) for face in range(3)]
    keep = root * (1.0 - settled - weights[0] - weights[1] - weights[2])
    fall = root * settled
    grown = root * cell_area
    fluxes = [grown * weight for weight in weights]

    for face in range(3):
        hot = jnp.where(
            lax.broadcasted_iota(jnp.int32, (cells, cells), 0) == slots[pl.ds(face, 1), :], one, zero
        )
        other = jnp.dot(v[...], hot, preferred_element_type=jnp.float32)
        for layer in range(layers):
            rows = pl.ds(layer * width, width)
            term = fluxes[face][layer : layer + 1] * other[layer * width : (layer + 1) * width]
            if face == 0:
                term = term + keep[layer : layer + 1] * probes[rows, :].astype(jnp.float32)
                if layer < layers - 1:
                    lower = probes[pl.ds((layer + 1) * width, width), :]
                    term = term + fall[layer : layer + 1] * lower.astype(jnp.float32)
                total[rows, :] = term
            else:
                total[rows, :] += term

    for arrival in arrivals:
        arrival.wait()

    for face in range(3):
        place = slots[pl.ds(face, 1), :] - cells
        hot = jnp.where(
            lax.broadcasted_iota(jnp.int32, (2 * halo, cells), 0) == place, one, zero
        )
        other = jnp.dot(ghosts[...], hot, preferred_element_type=jnp.float32)
        for layer in range(layers):
            rows = pl.ds(layer * width, width)
            term = fluxes[face][layer : layer + 1] * other[layer * width : (layer + 1) * width]
            term = total[rows, :] + term
            if face < 2:
                total[rows, :] = term
            else:
                high = term.astype(jnp.bfloat16)
                low = (term - high.astype(jnp.float32)).astype(jnp.bfloat16)
                pairs[layer // 2, pl.ds((layer % 2) * 2 * width, width), :] = high
                pairs[layer // 2, pl.ds((layer % 2) * 2 * width + width, width), :] = low

    square = None
    for pair in range(layers // 2):
        rows = pairs[pair]
        product = lax.dot_general(rows, rows, NT, preferred_element_type=jnp.float32)
        square = product if square is None else square + product
    w = width
    gram = None
    for layer in range(2):
        for a in range(2):
            for b in range(2):
                r, c = (2 * layer + a) * w, (2 * layer + b) * w
                piece = square[r : r + w, c : c + w]
                gram = piece if gram is None else gram + piece
    folded = jnp.concatenate([gram[: w // 2], gram[w // 2 :]], axis=1)
    halves[0] = folded[: w // 4]
    halves[1] = folded[w // 4 :]

    def send(phase, source, target, peers):
        for peer in peers:
            pltpu.make_async_remote_copy(
                src_ref=source,
                dst_ref=target,
                send_sem=send_sem.at[phase],
                recv_sem=recv_sem.at[phase],
                device_id=(peer,),
                device_id_type=MESH,
            ).start()

    def settle_all(buffer, count, semaphore):
        span = buffer.at[pl.ds(0, count)] if count else buffer
        pltpu.make_async_copy(span, span, semaphore).wait()

    def add_up(receive):
        terms = [receive[index] for index in range(receive.shape[0])]
        while len(terms) > 1:
            terms = [a + b for a, b in zip(terms[::2], terms[1::2])]
        return terms[0]

    send(0, halves.at[1 - core], from_core, [sibling])
    settle_all(from_core, 0, recv_sem.at[0])
    along_z[z] = halves[core] + from_core[...]
    send(1, along_z.at[z], along_z.at[z], z_peers)
    settle_all(along_z, Z - 1, recv_sem.at[1])
    along_xy[block] = add_up(along_z)
    send(2, along_xy.at[block], along_xy.at[block], xy_peers)
    settle_all(along_xy, X * Y - 1, recv_sem.at[2])
    final[core] = add_up(along_xy)
    send(3, final.at[core], final.at[core], [sibling])
    settle_all(from_core, 0, recv_sem.at[3])
    gram_out[...] = final[...]

    settle_all(from_core, 0, send_sem.at[0])
    settle_all(along_z, Z - 1, send_sem.at[1])
    settle_all(along_xy, X * Y - 1, send_sem.at[2])
    settle_all(from_core, 0, send_sem.at[3])
    for copy in copies:
        copy.wait_send()


def factorize(strips, width):
    full = (8, 2 * width)
    row = lax.broadcasted_iota(jnp.int32, full, 0)
    strips, finished = list(strips), []

    def lane(values, index):
        return jnp.take_along_axis(values, jnp.full(full, index, jnp.int32), axis=1)

    def line(values, index):
        return jnp.broadcast_to(values[index : index + 1], full)

    for home in range(width // 8):
        step = 8 * home
        mine = strips[home]
        upper = [line(mine, p) for p in range(8)]
        block = [[None] * 8 for _ in range(8)]
        for q in range(8):
            column = lane(mine, step + q)
            for p in range(q + 1):
                block[p][q] = line(column, p)
        ratio = [[None] * 8 for _ in range(8)]
        scaled = []
        for p in range(8):
            reciprocal = 1.0 / block[p][p]
            for q in range(p + 1, 8):
                ratio[q][p] = block[p][q] * reciprocal
            for q in range(p + 1, 8):
                for t in range(q, 8):
                    block[q][t] = block[q][t] - ratio[q][p] * block[p][t]
                upper[q] = upper[q] - ratio[q][p] * upper[p]
            scaled.append(upper[p] * reciprocal)
        for strip in range(home + 1, width // 8):
            columns = [lane(strips[strip], step + q) for q in range(8)]
            for p in range(8):
                for q in range(p + 1, 8):
                    columns[q] = columns[q] - ratio[q][p] * columns[p]
            terms = [c * n for c, n in zip(columns, scaled)]
            while len(terms) > 1:
                terms = [a + b for a, b in zip(terms[::2], terms[1::2])]
            strips[strip] = strips[strip] - terms[0]
        done = None
        for p in range(8):
            scaled_row = upper[p] / jnp.sqrt(block[p][p])
            done = scaled_row if done is None else jnp.where(row == p, scaled_row, done)
        finished.append(done)
    return finished


def basis_kernel(scale, pairs, gram, basis, factor, results, store_sem):
    groups = pairs.shape[0]
    width = factor.shape[0]
    folded = jnp.concatenate([gram[0], gram[1]], axis=0)
    whole = jnp.concatenate([folded[:, :width], folded[:, width:]], axis=0)
    unit = (lax.broadcasted_iota(jnp.int32, (width, width), 0)
            == lax.broadcasted_iota(jnp.int32, (width, width), 1)).astype(jnp.float32)
    work = jnp.concatenate([whole, unit], axis=1)
    work = jnp.concatenate(factorize([work[8 * i : 8 * i + 8] for i in range(width // 8)], width), axis=0)
    row = lax.broadcasted_iota(jnp.int32, (width, 2 * width), 0)
    lane = lax.broadcasted_iota(jnp.int32, (width, 2 * width), 1)
    factor[...] = jnp.where(lane >= row, work, 0.0)[:, :width] / scale
    inverse = jnp.where(lane - width <= row, work, 0.0)[:, width:] * scale
    high = inverse.astype(jnp.bfloat16)
    low = (inverse - high.astype(jnp.float32)).astype(jnp.bfloat16)
    none = jnp.zeros_like(high)

    def spread(block):
        return [
            jnp.concatenate([block, block, none, none], axis=1),
            jnp.concatenate([none, none, block, block], axis=1),
        ]

    stacked = jnp.concatenate(spread(high) + spread(low), axis=0)
    stores = []
    for group in range(groups):
        product = jnp.dot(stacked, pairs[group], preferred_element_type=jnp.float32)
        results[group] = product[: 2 * width] + product[2 * width :]
        copy = pltpu.make_async_copy(results.at[group], basis.at[group], store_sem.at[group])
        copy.start()
        stores.append(copy)
    for copy in stores:
        copy.wait()


def body(probes, area, settle, courant, orient, local_slot, send_rows):
    layers, width, cells = probes.shape
    halo = send_rows.shape[0] // 2
    devices = lax.axis_size("cells")
    groups = layers // 2
    vmem = pl.BlockSpec(memory_space=pltpu.VMEM)
    hbm = pl.BlockSpec(memory_space=pltpu.HBM)
    chunks = layers * width // CHUNK
    inputs = (
        probes.reshape(layers * width, cells), area[None, :], settle, courant, orient,
        local_slot, send_rows[None, :],
    )
    half = (width // 4, 2 * width)
    pairs, gram = pl.pallas_call(
        functools.partial(advect_kernel, devices),
        out_shape=(
            jax.ShapeDtypeStruct((groups, 4 * width, cells), jnp.bfloat16),
            jax.ShapeDtypeStruct((2, *half), jnp.float32),
        ),
        in_specs=[hbm] * 7,
        out_specs=(vmem, vmem),
        scratch_shapes=[pltpu.VMEM(array.shape, array.dtype) for array in inputs] + [
            pltpu.VMEM((layers * width, cells), jnp.bfloat16),
            pltpu.VMEM((2, layers * width, halo), jnp.bfloat16),
            pltpu.VMEM((layers * width, 2 * halo), jnp.bfloat16),
            pltpu.VMEM((layers * width, cells), jnp.float32),
            pltpu.VMEM((2, *half), jnp.float32),
            pltpu.VMEM(half, jnp.float32),
            pltpu.VMEM((Z, *half), jnp.float32),
            pltpu.VMEM((X * Y, *half), jnp.float32),
            pltpu.VMEM((2, *half), jnp.float32),
            pltpu.SemaphoreType.DMA((7,)),
            pltpu.SemaphoreType.DMA((2, chunks)),
            pltpu.SemaphoreType.DMA((2, chunks)),
            pltpu.SemaphoreType.DMA((4,)),
            pltpu.SemaphoreType.DMA((4,)),
        ],
        compiler_params=pltpu.CompilerParams(
            collective_id=0, has_side_effects=True, vmem_limit_bytes=44 * 2**20
        ),
        name="advect",
    )(*(pltpu.with_memory_space_constraint(array, pltpu.HBM) for array in inputs))
    scale = math.sqrt(layers * cells * devices)
    basis, factor = pl.pallas_call(
        functools.partial(basis_kernel, scale),
        out_shape=(
            jax.ShapeDtypeStruct((groups, 2 * width, cells), jnp.float32),
            jax.ShapeDtypeStruct((width, width), jnp.float32),
        ),
        in_specs=[vmem, vmem],
        out_specs=(hbm, vmem),
        scratch_shapes=[
            pltpu.VMEM((groups, 2 * width, cells), jnp.float32),
            pltpu.SemaphoreType.DMA((groups,)),
        ],
        compiler_params=pltpu.CompilerParams(vmem_limit_bytes=24 * 2**20),
        name="basis",
    )(pairs, gram)
    return basis.reshape(layers, width, cells), factor


def solution(mesh):
    in_specs = (
        P(None, None, "cells"),
        P("cells"),
        P(None, "cells"),
        P(None, None, "cells"),
        P(None, None, "cells"),
        P(None, "cells"),
        P("cells"),
    )
    out_specs = (P(None, None, "cells"), P())
    return jax.shard_map(body, mesh=mesh, in_specs=in_specs, out_specs=out_specs, check_vma=False)
```

time: 58.1 us -> 43.8 us (0.75)
  Pallas kernels: 50.6 us -> 42.8 us
  local copies, waits for them, and re-layouts: 6.36 us -> 0 us
    unnamed x14 -> x0, local copies, waits for them, and re-layouts: 6.36 us -> none
    pallas_call x1, Pallas kernels: 10.1 us -> 4.74 us  [body(): pl.pallas_call(functools.partial(basis_kernel, scale), out_shape=(jax.Sha...]
    pallas_call x1, Pallas kernels: 40.6 us -> 38.1 us  [body(): pl.pallas_call(functools.partial(advect_kernel, devices), out_shape=(jax....]
where the time goes in v2:
time: 43.8 us; the launch traced here: 43.6 us
  Pallas kernels  42.8 us (98%)
  between operations  0.8 us (2%)
    pallas_call x1, Pallas kernels, body(): pl.pallas_call(functools.partial(advect_kernel, devices), out_shape=(jax....  38.1 us
    pallas_call x1, Pallas kernels, body(): pl.pallas_call(functools.partial(basis_kernel, scale), out_shape=(jax.Sha...  4.74 us

profile of v2, /device:TPU:1, one launch (start us, length us, event | category | flops | bytes accessed | tf_op | source)
XLA Modules:
  0.0 43.6 jit_solution(2432227665457476467)
XLA Ops:
  0.6 38.1 %advect.1 = (bf16[8,256,1024]{2,1,0:T(8,128)(2,1)S(1)}, f32[2,16,128]{2,1,0:T(8,128)S(1)}) custom-call(bf16[1024,1024]{1,0:T(8,128)(2,1)} %bitcast.4, f32[1,1024]{1,0:T(1,128)} %bitcast.5, f32[16,1024]{1,0:T(8,128)} %settle_in.1, f32[3,16,1024]{2,1,0:T(8,128)} %courant_in.1, s32[3,16,1024]{2,1,0:T(8,128)} %orient_in.1, s32[3,1024]{1,0:T(4,128)} %slots_in.1, ...), custom_call_target="tpu_custom_call" | custom-call | tf_op jit(solution)/shard_map/advect/pallas_call | solution.py:298
  38.7 4.7 %basis.1 = (f32[8,128,1024]{2,1,0:T(8,128)}, f32[64,64]{1,0:T(8,128)}) custom-call(bf16[8,256,1024]{2,1,0:T(8,128)(2,1)S(1)} %get-tuple-element.6.pairs, f32[2,16,128]{2,1,0:T(8,128)S(1)} %get-tuple-element.7.gram), custom_call_target="tpu_custom_call" | custom-call | tf_op jit(solution)/shard_map/basis/pallas_call | solution.py:328

commit v3 on v2

--- a/solution.py
+++ b/solution.py
@@ -11,7 +11,8 @@
 
 MESH = pl.DeviceIdType.MESH
 Y, X, Z = 4, 4, 8
-CHUNK = 512
+SENT = (128, 128, 256, 256, 256)
+CHUNK = 256
 NT = (((1,), (1,)), ((), ()))
 
 
@@ -26,13 +27,12 @@
     devices, probes_in, area_in, settle_in, courant_in, orient_in, slots_in, sends_in,
     pairs, gram_out,
     probes, area, settle, courant, orient, slots, sends,
-    v, outgoing, ghosts, total, halves, from_core, along_z, along_xy, final,
+    v, outgoing, ghosts, hots, total, halves, from_core, along_z, along_xy, final,
     load_sem, halo_send, halo_recv, send_sem, recv_sem,
 ):
     layers, cells = settle.shape
     width = probes.shape[0] // layers
     halo = sends.shape[1] // 2
-    chunks = probes.shape[0] // CHUNK
     me = lax.axis_index("cells")
     left, right = lax.rem(me + devices - 1, devices), lax.rem(me + 1, devices)
     core, z, block = lax.rem(me, 2), lax.rem(me // 2, Z), me // (2 * Z)
@@ -45,11 +45,15 @@
     ]
 
     loads = {}
-    for index, (name, source, target) in enumerate((
-        ("sends", sends_in, sends), ("area", area_in, area), ("probes", probes_in, probes),
+    starts = [sum(SENT[:chunk]) for chunk in range(len(SENT))]
+    spans = [pl.ds(start, size) for start, size in zip(starts, SENT)]
+    plan = [("sends", sends_in, sends), ("area", area_in, area)]
+    plan += [(chunk, probes_in.at[span], probes.at[span]) for chunk, span in enumerate(spans)]
+    plan += [
         ("slots", slots_in, slots), ("courant", courant_in, courant),
         ("orient", orient_in, orient), ("settle", settle_in, settle),
-    )):
+    ]
+    for index, (name, source, target) in enumerate(plan):
         loads[name] = pltpu.make_async_copy(source, target, load_sem.at[index])
         loads[name].start()
 
@@ -66,10 +70,9 @@
     loads["area"].wait()
     cell_area = area[...]
     inverse_area = 1.0 / cell_area
-    loads["probes"].wait()
     copies, arrivals = [], []
-    for chunk in range(chunks):
-        rows = pl.ds(chunk * CHUNK, CHUNK)
+    for chunk, rows in enumerate(spans):
+        loads[chunk].wait()
         part = (probes[rows, :].astype(jnp.float32) * inverse_area).astype(jnp.bfloat16)
         v[rows, :] = part
         picked = jnp.dot(part, pick, preferred_element_type=jnp.float32).astype(jnp.bfloat16)
@@ -106,6 +109,10 @@
         hot = jnp.where(
             lax.broadcasted_iota(jnp.int32, (cells, cells), 0) == slots[pl.ds(face, 1), :], one, zero
         )
+        place = slots[pl.ds(face, 1), :] - cells
+        hots[face] = jnp.where(
+            lax.broadcasted_iota(jnp.int32, (2 * halo, cells), 0) == place, one, zero
+        )
         other = jnp.dot(v[...], hot, preferred_element_type=jnp.float32)
         for layer in range(layers):
             rows = pl.ds(layer * width, width)
@@ -119,32 +126,35 @@
             else:
                 total[rows, :] += term
 
+    def square_of(chunk):
+        first = chunk * CHUNK // (2 * width)
+        product = None
+        for pair in range(first, first + CHUNK // (2 * width)):
+            rows = pairs[pair]
+            term = lax.dot_general(rows, rows, NT, preferred_element_type=jnp.float32)
+            product = term if product is None else product + term
+        return product
+
     for arrival in arrivals:
         arrival.wait()
-
-    for face in range(3):
-        place = slots[pl.ds(face, 1), :] - cells
-        hot = jnp.where(
-            lax.broadcasted_iota(jnp.int32, (2 * halo, cells), 0) == place, one, zero
-        )
-        other = jnp.dot(ghosts[...], hot, preferred_element_type=jnp.float32)
-        for layer in range(layers):
-            rows = pl.ds(layer * width, width)
-            term = fluxes[face][layer : layer + 1] * other[layer * width : (layer + 1) * width]
-            term = total[rows, :] + term
-            if face < 2:
-                total[rows, :] = term
-            else:
-                high = term.astype(jnp.bfloat16)
-                low = (term - high.astype(jnp.float32)).astype(jnp.bfloat16)
-                pairs[layer // 2, pl.ds((layer % 2) * 2 * width, width), :] = high
-                pairs[layer // 2, pl.ds((layer % 2) * 2 * width + width, width), :] = low
-
     square = None
-    for pair in range(layers // 2):
-        rows = pairs[pair]
-        product = lax.dot_general(rows, rows, NT, preferred_element_type=jnp.float32)
-        square = product if square is None else square + product
+    for chunk in range(probes.shape[0] // CHUNK):
+        rows = ghosts[pl.ds(chunk * CHUNK, CHUNK), :]
+        others = [jnp.dot(rows, hots[face], preferred_element_type=jnp.float32) for face in range(3)]
+        if chunk:
+            product = square_of(chunk - 1)
+            square = product if square is None else square + product
+        for inner in range(CHUNK // width):
+            layer = chunk * (CHUNK // width) + inner
+            term = total[pl.ds(layer * width, width), :]
+            for face in range(3):
+                other = others[face][inner * width : (inner + 1) * width]
+                term = term + fluxes[face][layer : layer + 1] * other
+            high = term.astype(jnp.bfloat16)
+            low = (term - high.astype(jnp.float32)).astype(jnp.bfloat16)
+            pairs[layer // 2, pl.ds((layer % 2) * 2 * width, width), :] = high
+            pairs[layer // 2, pl.ds((layer % 2) * 2 * width + width, width), :] = low
+    square = square + square_of(probes.shape[0] // CHUNK - 1)
     w = width
     gram = None
     for layer in range(2):
@@ -289,7 +299,7 @@
     groups = layers // 2
     vmem = pl.BlockSpec(memory_space=pltpu.VMEM)
     hbm = pl.BlockSpec(memory_space=pltpu.HBM)
-    chunks = layers * width // CHUNK
+    sent = len(SENT)
     inputs = (
         probes.reshape(layers * width, cells), area[None, :], settle, courant, orient,
         local_slot, send_rows[None, :],
@@ -307,15 +317,16 @@
             pltpu.VMEM((layers * width, cells), jnp.bfloat16),
             pltpu.VMEM((2, layers * width, halo), jnp.bfloat16),
             pltpu.VMEM((layers * width, 2 * halo), jnp.bfloat16),
+            pltpu.VMEM((3, 2 * halo, cells), jnp.bfloat16),
             pltpu.VMEM((layers * width, cells), jnp.float32),
             pltpu.VMEM((2, *half), jnp.float32),
             pltpu.VMEM(half, jnp.float32),
             pltpu.VMEM((Z, *half), jnp.float32),
             pltpu.VMEM((X * Y, *half), jnp.float32),
             pltpu.VMEM((2, *half), jnp.float32),
-            pltpu.SemaphoreType.DMA((7,)),
-            pltpu.SemaphoreType.DMA((2, chunks)),
-            pltpu.SemaphoreType.DMA((2, chunks)),
+            pltpu.SemaphoreType.DMA((6 + sent,)),
+            pltpu.SemaphoreType.DMA((2, sent)),
+            pltpu.SemaphoreType.DMA((2, sent)),
             pltpu.SemaphoreType.DMA((4,)),
             pltpu.SemaphoreType.DMA((4,)),
         ],

time: 43.8 us -> 43.3 us (0.989)
  no operation moved by 1% of the time
where the time goes in v3:
time: 43.3 us; the launch traced here: 43.2 us
  Pallas kernels  42.4 us (98%)
  between operations  0.8 us (2%)
    pallas_call x1, Pallas kernels, body(): pl.pallas_call(functools.partial(advect_kernel, devices), out_shape=(jax....  37.7 us
    pallas_call x1, Pallas kernels, body(): pl.pallas_call(functools.partial(basis_kernel, scale), out_shape=(jax.Sha...  4.74 us

profile of v3, /device:TPU:1, one launch (start us, length us, event | category | flops | bytes accessed | tf_op | source)
XLA Modules:
  0.0 43.2 jit_solution(1108026076595040518)
XLA Ops:
  0.6 37.7 %advect.1 = (bf16[8,256,1024]{2,1,0:T(8,128)(2,1)S(1)}, f32[2,16,128]{2,1,0:T(8,128)S(1)}) custom-call(bf16[1024,1024]{1,0:T(8,128)(2,1)} %bitcast.4, f32[1,1024]{1,0:T(1,128)} %bitcast.5, f32[16,1024]{1,0:T(8,128)} %settle_in.1, f32[3,16,1024]{2,1,0:T(8,128)} %courant_in.1, s32[3,16,1024]{2,1,0:T(8,128)} %orient_in.1, s32[3,1024]{1,0:T(4,128)} %slots_in.1, ...), custom_call_target="tpu_custom_call" | custom-call | tf_op jit(solution)/shard_map/advect/pallas_call | solution.py:308
  38.3 4.7 %basis.1 = (f32[8,128,1024]{2,1,0:T(8,128)}, f32[64,64]{1,0:T(8,128)}) custom-call(bf16[8,256,1024]{2,1,0:T(8,128)(2,1)S(1)} %get-tuple-element.6.pairs, f32[2,16,128]{2,1,0:T(8,128)S(1)} %get-tuple-element.7.gram), custom_call_target="tpu_custom_call" | custom-call | tf_op jit(solution)/shard_map/basis/pallas_call | solution.py:339

commit v4 on v3

--- a/solution.py
+++ b/solution.py
@@ -11,8 +11,9 @@
 
 MESH = pl.DeviceIdType.MESH
 Y, X, Z = 4, 4, 8
-SENT = (128, 128, 256, 256, 256)
+SENT = (256, 768)
 CHUNK = 256
+PARTS = 2
 NT = (((1,), (1,)), ((), ()))
 
 
@@ -34,10 +35,10 @@
     width = probes.shape[0] // layers
     halo = sends.shape[1] // 2
     me = lax.axis_index("cells")
-    left, right = lax.rem(me + devices - 1, devices), lax.rem(me + 1, devices)
     core, z, block = lax.rem(me, 2), lax.rem(me // 2, Z), me // (2 * Z)
     y, x = block // X, lax.rem(block, X)
     sibling = me + 1 - 2 * core
+    distant = lax.rem(me + devices + 2 * core - 1, devices)
     z_peers = [me + 2 * (lax.rem(z + step, Z) - z) for step in far_first(Z)]
     xy_peers = [
         (lax.rem(y + dy, Y) * X + lax.rem(x + dx, X)) * 2 * Z + z * 2 + core
@@ -58,7 +59,7 @@
         loads[name].start()
 
     barrier = pltpu.get_barrier_semaphore()
-    greeted = [left, right, sibling] + z_peers + xy_peers
+    greeted = [sibling, distant] + z_peers + xy_peers
     for peer in greeted:
         pl.semaphore_signal(barrier, inc=1, device_id=(peer,), device_id_type=MESH)
 
@@ -70,7 +71,7 @@
     loads["area"].wait()
     cell_area = area[...]
     inverse_area = 1.0 / cell_area
-    copies, arrivals = [], []
+    copies = []
     for chunk, rows in enumerate(spans):
         loads[chunk].wait()
         part = (probes[rows, :].astype(jnp.float32) * inverse_area).astype(jnp.bfloat16)
@@ -80,20 +81,24 @@
         outgoing[1, rows, :] = picked[:, halo:]
         if chunk == 0:
             pl.semaphore_wait(barrier, len(greeted))
-        for side, target in ((0, left), (1, right)):
-            copy = pltpu.make_async_remote_copy(
-                src_ref=outgoing.at[side, rows, :],
-                dst_ref=ghosts.at[rows, pl.ds((1 - side) * halo, halo)],
-                send_sem=halo_send.at[side, chunk],
-                recv_sem=halo_recv.at[1 - side, chunk],
-                device_id=(target,),
-                device_id_type=MESH,
-            )
-            copy.start()
-            copies.append(copy)
-            arrivals.append(pltpu.make_async_copy(
-                outgoing.at[side, rows, :], ghosts.at[rows, pl.ds(side * halo, halo)], halo_recv.at[side, chunk]
-            ))
+        copies.append(pltpu.make_async_remote_copy(
+            src_ref=outgoing.at[core, rows, :],
+            dst_ref=ghosts.at[1, rows, :],
+            send_sem=halo_send.at[chunk],
+            recv_sem=halo_recv.at[chunk],
+            device_id=(distant,),
+            device_id_type=MESH,
+        ))
+        copies[-1].start()
+    beside = pltpu.make_async_remote_copy(
+        src_ref=outgoing.at[1 - core],
+        dst_ref=ghosts.at[0],
+        send_sem=halo_send.at[len(SENT)],
+        recv_sem=halo_recv.at[len(SENT)],
+        device_id=(sibling,),
+        device_id_type=MESH,
+    )
+    beside.start()
 
     for name in ("slots", "courant", "orient", "settle"):
         loads[name].wait()
@@ -109,10 +114,11 @@
         hot = jnp.where(
             lax.broadcasted_iota(jnp.int32, (cells, cells), 0) == slots[pl.ds(face, 1), :], one, zero
         )
-        place = slots[pl.ds(face, 1), :] - cells
-        hots[face] = jnp.where(
-            lax.broadcasted_iota(jnp.int32, (2 * halo, cells), 0) == place, one, zero
-        )
+        for kind, side in ((0, 1 - core), (1, core)):
+            place = slots[pl.ds(face, 1), :] - cells - side * halo
+            hots[kind, face] = jnp.where(
+                lax.broadcasted_iota(jnp.int32, (halo, cells), 0) == place, one, zero
+            )
         other = jnp.dot(v[...], hot, preferred_element_type=jnp.float32)
         for layer in range(layers):
             rows = pl.ds(layer * width, width)
@@ -135,12 +141,18 @@
             product = term if product is None else product + term
         return product
 
-    for arrival in arrivals:
-        arrival.wait()
+    beside.wait_recv()
+    for face in range(3):
+        other = jnp.dot(ghosts[0], hots[0, face], preferred_element_type=jnp.float32)
+        for layer in range(layers):
+            rows = pl.ds(layer * width, width)
+            total[rows, :] += fluxes[face][layer : layer + 1] * other[layer * width : (layer + 1) * width]
+    for copy in copies:
+        copy.wait_recv()
     square = None
     for chunk in range(probes.shape[0] // CHUNK):
-        rows = ghosts[pl.ds(chunk * CHUNK, CHUNK), :]
-        others = [jnp.dot(rows, hots[face], preferred_element_type=jnp.float32) for face in range(3)]
+        rows = ghosts[1, pl.ds(chunk * CHUNK, CHUNK), :]
+        others = [jnp.dot(rows, hots[1, face], preferred_element_type=jnp.float32) for face in range(3)]
         if chunk:
             product = square_of(chunk - 1)
             square = product if square is None else square + product
@@ -205,14 +217,14 @@
     settle_all(along_z, Z - 1, send_sem.at[1])
     settle_all(along_xy, X * Y - 1, send_sem.at[2])
     settle_all(from_core, 0, send_sem.at[3])
-    for copy in copies:
+    for copy in copies + [beside]:
         copy.wait_send()
 
 
 def factorize(strips, width):
     full = (8, 2 * width)
     row = lax.broadcasted_iota(jnp.int32, full, 0)
-    strips, finished = list(strips), []
+    strips = list(strips)
 
     def lane(values, index):
         return jnp.take_along_axis(values, jnp.full(full, index, jnp.int32), axis=1)
@@ -253,41 +265,47 @@
         for p in range(8):
             scaled_row = upper[p] / jnp.sqrt(block[p][p])
             done = scaled_row if done is None else jnp.where(row == p, scaled_row, done)
-        finished.append(done)
-    return finished
+        yield done
 
 
 def basis_kernel(scale, pairs, gram, basis, factor, results, store_sem):
     groups = pairs.shape[0]
     width = factor.shape[0]
+    part = width // PARTS
     folded = jnp.concatenate([gram[0], gram[1]], axis=0)
     whole = jnp.concatenate([folded[:, :width], folded[:, width:]], axis=0)
     unit = (lax.broadcasted_iota(jnp.int32, (width, width), 0)
             == lax.broadcasted_iota(jnp.int32, (width, width), 1)).astype(jnp.float32)
     work = jnp.concatenate([whole, unit], axis=1)
-    work = jnp.concatenate(factorize([work[8 * i : 8 * i + 8] for i in range(width // 8)], width), axis=0)
-    row = lax.broadcasted_iota(jnp.int32, (width, 2 * width), 0)
-    lane = lax.broadcasted_iota(jnp.int32, (width, 2 * width), 1)
-    factor[...] = jnp.where(lane >= row, work, 0.0)[:, :width] / scale
-    inverse = jnp.where(lane - width <= row, work, 0.0)[:, width:] * scale
-    high = inverse.astype(jnp.bfloat16)
-    low = (inverse - high.astype(jnp.float32)).astype(jnp.bfloat16)
-    none = jnp.zeros_like(high)
-
-    def spread(block):
-        return [
-            jnp.concatenate([block, block, none, none], axis=1),
-            jnp.concatenate([none, none, block, block], axis=1),
-        ]
-
-    stacked = jnp.concatenate(spread(high) + spread(low), axis=0)
+    finished = factorize([work[8 * i : 8 * i + 8] for i in range(width // 8)], width)
+    row = lax.broadcasted_iota(jnp.int32, (part, 2 * width), 0)
+    lane = lax.broadcasted_iota(jnp.int32, (part, 2 * width), 1)
+    none = jnp.zeros((part, width), jnp.bfloat16)
     stores = []
-    for group in range(groups):
-        product = jnp.dot(stacked, pairs[group], preferred_element_type=jnp.float32)
-        results[group] = product[: 2 * width] + product[2 * width :]
-        copy = pltpu.make_async_copy(results.at[group], basis.at[group], store_sem.at[group])
-        copy.start()
-        stores.append(copy)
+    for index in range(PARTS):
+        first = index * part
+        rows = jnp.concatenate([next(finished) for _ in range(part // 8)], axis=0)
+        factor[pl.ds(first, part), :] = jnp.where(lane >= row + first, rows, 0.0)[:, :width] / scale
+        inverse = jnp.where(lane - width <= row + first, rows, 0.0)[:, width:] * scale
+        high = inverse.astype(jnp.bfloat16)
+        low = (inverse - high.astype(jnp.float32)).astype(jnp.bfloat16)
+        stacked = jnp.concatenate([
+            jnp.concatenate(blocks, axis=1)
+            for value in (high, low)
+            for blocks in ([value, value, none, none], [none, none, value, value])
+        ], axis=0)
+        for group in range(groups):
+            product = jnp.dot(stacked, pairs[group], preferred_element_type=jnp.float32)
+            product = product[: 2 * part] + product[2 * part :]
+            for layer in range(2):
+                target = pl.ds(layer * width + first, part)
+                results[group, target, :] = product[layer * part : (layer + 1) * part]
+                copy = pltpu.make_async_copy(
+                    results.at[group, target, :], basis.at[group, target, :],
+                    store_sem.at[index, 2 * group + layer],
+                )
+                copy.start()
+                stores.append(copy)
     for copy in stores:
         copy.wait()
 
@@ -316,8 +334,8 @@
         scratch_shapes=[pltpu.VMEM(array.shape, array.dtype) for array in inputs] + [
             pltpu.VMEM((layers * width, cells), jnp.bfloat16),
             pltpu.VMEM((2, layers * width, halo), jnp.bfloat16),
-            pltpu.VMEM((layers * width, 2 * halo), jnp.bfloat16),
-            pltpu.VMEM((3, 2 * halo, cells), jnp.bfloat16),
+            pltpu.VMEM((2, layers * width, halo), jnp.bfloat16),
+            pltpu.VMEM((2, 3, halo, cells), jnp.bfloat16),
             pltpu.VMEM((layers * width, cells), jnp.float32),
             pltpu.VMEM((2, *half), jnp.float32),
             pltpu.VMEM(half, jnp.float32),
@@ -325,8 +343,8 @@
             pltpu.VMEM((X * Y, *half), jnp.float32),
             pltpu.VMEM((2, *half), jnp.float32),
             pltpu.SemaphoreType.DMA((6 + sent,)),
-            pltpu.SemaphoreType.DMA((2, sent)),
-            pltpu.SemaphoreType.DMA((2, sent)),
+            pltpu.SemaphoreType.DMA((sent + 1,)),
+            pltpu.SemaphoreType.DMA((sent + 1,)),
             pltpu.SemaphoreType.DMA((4,)),
             pltpu.SemaphoreType.DMA((4,)),
         ],
@@ -346,7 +364,7 @@
         out_specs=(hbm, vmem),
         scratch_shapes=[
             pltpu.VMEM((groups, 2 * width, cells), jnp.float32),
-            pltpu.SemaphoreType.DMA((groups,)),
+            pltpu.SemaphoreType.DMA((PARTS, layers)),
         ],
         compiler_params=pltpu.CompilerParams(vmem_limit_bytes=24 * 2**20),
         name="basis",

time: 43.3 us -> 42.3 us (0.977)
  Pallas kernels: 42.4 us -> 41.4 us
    pallas_call x1, Pallas kernels: 37.7 us -> 37 us  [body(): pl.pallas_call(functools.partial(advect_kernel, devices), out_shape=(jax....]
where the time goes in v4:
time: 42.3 us; the launch traced here: 42.2 us
  Pallas kernels  41.4 us (98%)
  between operations  0.8 us (2%)
    pallas_call x1, Pallas kernels, body(): pl.pallas_call(functools.partial(advect_kernel, devices), out_shape=(jax....  37 us
    pallas_call x1, Pallas kernels, body(): pl.pallas_call(functools.partial(basis_kernel, scale), out_shape=(jax.Sha...  4.42 us

profile of v4, /device:TPU:1, one launch (start us, length us, event | category | flops | bytes accessed | tf_op | source)
XLA Modules:
  0.0 42.2 jit_solution(17160107715495716312)
XLA Ops:
  0.6 37.0 %advect.1 = (bf16[8,256,1024]{2,1,0:T(8,128)(2,1)S(1)}, f32[2,16,128]{2,1,0:T(8,128)S(1)}) custom-call(bf16[1024,1024]{1,0:T(8,128)(2,1)} %bitcast.4, f32[1,1024]{1,0:T(1,128)} %bitcast.5, f32[16,1024]{1,0:T(8,128)} %settle_in.1, f32[3,16,1024]{2,1,0:T(8,128)} %courant_in.1, s32[3,16,1024]{2,1,0:T(8,128)} %orient_in.1, s32[3,1024]{1,0:T(4,128)} %slots_in.1, ...), custom_call_target="tpu_custom_call" | custom-call | tf_op jit(solution)/shard_map/advect/pallas_call | solution.py:326
  37.6 4.4 %basis.1 = (f32[8,128,1024]{2,1,0:T(8,128)}, f32[64,64]{1,0:T(8,128)}) custom-call(bf16[8,256,1024]{2,1,0:T(8,128)(2,1)S(1)} %get-tuple-element.6.pairs, f32[2,16,128]{2,1,0:T(8,128)S(1)} %get-tuple-element.7.gram), custom_call_target="tpu_custom_call" | custom-call | tf_op jit(solution)/shard_map/basis/pallas_call | solution.py:357

commit v5 on v4

--- a/solution.py
+++ b/solution.py
@@ -11,8 +11,8 @@
 
 MESH = pl.DeviceIdType.MESH
 Y, X, Z = 4, 4, 8
-SENT = (256, 768)
-CHUNK = 256
+SENT = (512, 512)
+CHUNKS = (256, 256, 256, 128, 128)
 PARTS = 2
 NT = (((1,), (1,)), ((), ()))
 
@@ -50,18 +50,22 @@
     spans = [pl.ds(start, size) for start, size in zip(starts, SENT)]
     plan = [("sends", sends_in, sends), ("area", area_in, area)]
     plan += [(chunk, probes_in.at[span], probes.at[span]) for chunk, span in enumerate(spans)]
+    urgent = len(plan)
     plan += [
         ("slots", slots_in, slots), ("courant", courant_in, courant),
         ("orient", orient_in, orient), ("settle", settle_in, settle),
     ]
     for index, (name, source, target) in enumerate(plan):
         loads[name] = pltpu.make_async_copy(source, target, load_sem.at[index])
+    for name, _, _ in plan[:urgent]:
         loads[name].start()
 
     barrier = pltpu.get_barrier_semaphore()
     greeted = [sibling, distant] + z_peers + xy_peers
     for peer in greeted:
         pl.semaphore_signal(barrier, inc=1, device_id=(peer,), device_id_type=MESH)
+    for name, _, _ in plan[urgent:]:
+        loads[name].start()
 
     one, zero = jnp.bfloat16(1), jnp.bfloat16(0)
     loads["sends"].wait()
@@ -132,10 +136,9 @@
             else:
                 total[rows, :] += term
 
-    def square_of(chunk):
-        first = chunk * CHUNK // (2 * width)
+    def square_of(start, size):
         product = None
-        for pair in range(first, first + CHUNK // (2 * width)):
+        for pair in range(start // (2 * width), (start + size) // (2 * width)):
             rows = pairs[pair]
             term = lax.dot_general(rows, rows, NT, preferred_element_type=jnp.float32)
             product = term if product is None else product + term
@@ -150,14 +153,15 @@
     for copy in copies:
         copy.wait_recv()
     square = None
-    for chunk in range(probes.shape[0] // CHUNK):
-        rows = ghosts[1, pl.ds(chunk * CHUNK, CHUNK), :]
+    blocks = [(sum(CHUNKS[:index]), size) for index, size in enumerate(CHUNKS)]
+    for index, (start, size) in enumerate(blocks):
+        rows = ghosts[1, pl.ds(start, size), :]
         others = [jnp.dot(rows, hots[1, face], preferred_element_type=jnp.float32) for face in range(3)]
-        if chunk:
-            product = square_of(chunk - 1)
+        if index:
+            product = square_of(*blocks[index - 1])
             square = product if square is None else square + product
-        for inner in range(CHUNK // width):
-            layer = chunk * (CHUNK // width) + inner
+        for inner in range(size // width):
+            layer = start // width + inner
             term = total[pl.ds(layer * width, width), :]
             for face in range(3):
                 other = others[face][inner * width : (inner + 1) * width]
@@ -166,7 +170,7 @@
             low = (term - high.astype(jnp.float32)).astype(jnp.bfloat16)
             pairs[layer // 2, pl.ds((layer % 2) * 2 * width, width), :] = high
             pairs[layer // 2, pl.ds((layer % 2) * 2 * width + width, width), :] = low
-    square = square + square_of(probes.shape[0] // CHUNK - 1)
+    square = square + square_of(*blocks[-1])
     w = width
     gram = None
     for layer in range(2):

time: 42.3 us -> 41.5 us (0.981)
  Pallas kernels: 41.4 us -> 40.6 us
    pallas_call x1, Pallas kernels: 37 us -> 36.2 us  [body(): pl.pallas_call(functools.partial(advect_kernel, devices), out_shape=(jax....]
where the time goes in v5:
time: 41.5 us; the launch traced here: 41.4 us
  Pallas kernels  40.6 us (98%)
  between operations  0.8 us (2%)
    pallas_call x1, Pallas kernels, body(): pl.pallas_call(functools.partial(advect_kernel, devices), out_shape=(jax....  36.2 us
    pallas_call x1, Pallas kernels, body(): pl.pallas_call(functools.partial(basis_kernel, scale), out_shape=(jax.Sha...  4.42 us

profile of v5, /device:TPU:1, one launch (start us, length us, event | category | flops | bytes accessed | tf_op | source)
XLA Modules:
  0.0 41.4 jit_solution(17262891342825084307)
XLA Ops:
  0.6 36.2 %advect.1 = (bf16[8,256,1024]{2,1,0:T(8,128)(2,1)S(1)}, f32[2,16,128]{2,1,0:T(8,128)S(1)}) custom-call(bf16[1024,1024]{1,0:T(8,128)(2,1)} %bitcast.4, f32[1,1024]{1,0:T(1,128)} %bitcast.5, f32[16,1024]{1,0:T(8,128)} %settle_in.1, f32[3,16,1024]{2,1,0:T(8,128)} %courant_in.1, s32[3,16,1024]{2,1,0:T(8,128)} %orient_in.1, s32[3,1024]{1,0:T(4,128)} %slots_in.1, ...), custom_call_target="tpu_custom_call" | custom-call | tf_op jit(solution)/shard_map/advect/pallas_call | solution.py:330
  36.9 4.4 %basis.1 = (f32[8,128,1024]{2,1,0:T(8,128)}, f32[64,64]{1,0:T(8,128)}) custom-call(bf16[8,256,1024]{2,1,0:T(8,128)(2,1)S(1)} %get-tuple-element.6.pairs, f32[2,16,128]{2,1,0:T(8,128)S(1)} %get-tuple-element.7.gram), custom_call_target="tpu_custom_call" | custom-call | tf_op jit(solution)/shard_map/basis/pallas_call | solution.py:361

commit v6 on v5

--- a/solution.py
+++ b/solution.py
@@ -301,15 +301,14 @@
         for group in range(groups):
             product = jnp.dot(stacked, pairs[group], preferred_element_type=jnp.float32)
             product = product[: 2 * part] + product[2 * part :]
+            target = pl.ds(first, part)
             for layer in range(2):
-                target = pl.ds(layer * width + first, part)
-                results[group, target, :] = product[layer * part : (layer + 1) * part]
-                copy = pltpu.make_async_copy(
-                    results.at[group, target, :], basis.at[group, target, :],
-                    store_sem.at[index, 2 * group + layer],
-                )
-                copy.start()
-                stores.append(copy)
+                results[group, layer, target, :] = product[layer * part : (layer + 1) * part]
+            copy = pltpu.make_async_copy(
+                results.at[group, :, target, :], basis.at[group, :, target, :], store_sem.at[index, group]
+            )
+            copy.start()
+            stores.append(copy)
     for copy in stores:
         copy.wait()
 
@@ -361,14 +360,14 @@
     basis, factor = pl.pallas_call(
         functools.partial(basis_kernel, scale),
         out_shape=(
-            jax.ShapeDtypeStruct((groups, 2 * width, cells), jnp.float32),
+            jax.ShapeDtypeStruct((groups, 2, width, cells), jnp.float32),
             jax.ShapeDtypeStruct((width, width), jnp.float32),
         ),
         in_specs=[vmem, vmem],
         out_specs=(hbm, vmem),
         scratch_shapes=[
-            pltpu.VMEM((groups, 2 * width, cells), jnp.float32),
-            pltpu.SemaphoreType.DMA((PARTS, layers)),
+            pltpu.VMEM((groups, 2, width, cells), jnp.float32),
+            pltpu.SemaphoreType.DMA((PARTS, groups)),
         ],
         compiler_params=pltpu.CompilerParams(vmem_limit_bytes=24 * 2**20),
         name="basis",

time: 41.5 us -> 41.4 us (level)
  no operation moved by 1% of the time
where the time goes in v6:
time: 41.4 us; the launch traced here: 41.3 us
  Pallas kernels  40.5 us (98%)
  between operations  0.8 us (2%)
    pallas_call x1, Pallas kernels, body(): pl.pallas_call(functools.partial(advect_kernel, devices), out_shape=(jax....  36.2 us
    pallas_call x1, Pallas kernels, body(): pl.pallas_call(functools.partial(basis_kernel, scale), out_shape=(jax.Sha...  4.29 us

profile of v6, /device:TPU:1, one launch (start us, length us, event | category | flops | bytes accessed | tf_op | source)
XLA Modules:
  0.0 41.3 jit_solution(5195407391471386042)
XLA Ops:
  0.6 36.2 %advect.1 = (bf16[8,256,1024]{2,1,0:T(8,128)(2,1)S(1)}, f32[2,16,128]{2,1,0:T(8,128)S(1)}) custom-call(bf16[1024,1024]{1,0:T(8,128)(2,1)} %bitcast.4, f32[1,1024]{1,0:T(1,128)} %bitcast.5, f32[16,1024]{1,0:T(8,128)} %settle_in.1, f32[3,16,1024]{2,1,0:T(8,128)} %courant_in.1, s32[3,16,1024]{2,1,0:T(8,128)} %orient_in.1, s32[3,1024]{1,0:T(4,128)} %slots_in.1, ...), custom_call_target="tpu_custom_call" | custom-call | tf_op jit(solution)/shard_map/advect/pallas_call | solution.py:329
  36.9 4.3 %basis.1 = (f32[8,2,64,1024]{3,2,1,0:T(8,128)}, f32[64,64]{1,0:T(8,128)}) custom-call(bf16[8,256,1024]{2,1,0:T(8,128)(2,1)S(1)} %get-tuple-element.6.pairs, f32[2,16,128]{2,1,0:T(8,128)S(1)} %get-tuple-element.7.gram), custom_call_target="tpu_custom_call" | custom-call | tf_op jit(solution)/shard_map/basis/pallas_call | solution.py:360
